TPU v7x, 256 devices: a whole 4x4x8 slice. The times are simulated.
256 devices in a mesh: tower: 2 (over z_hi), seq: 64 (over x, z_lo, y), rep: 2 (over core).
Axes of the slice: x: 4, y: 4, z: 8 (z_hi: 2, z_lo: 4; z = z_hi * 4 + z_lo), core: 2. Of those that a mesh axis runs over, the one named last changes fastest.
Arguments:
- query_rows: bfloat16 [2, 2, 16384, 1536], P('tower', 'rep', 'seq'), may hold values from -130 to 130
- key_rows: bfloat16 [2, 2, 16384, 1536], P('tower', 'rep', 'seq'), may hold values from -4 to 4
- value_rows: bfloat16 [2, 2, 16384, 1536], P('tower', 'rep', 'seq'), may hold values from -6 to 6
- out_grad: bfloat16 [2, 2, 16384, 1536], P('tower', 'rep', 'seq'), may hold values from -12 to 12
- query_gain: float32 [2, 1536], P('tower'), may hold values from 0.5 to 2
- live_counts: int32 [2, 64], replicated, may hold values from 128 to 256, as said below
- intersection: int32 [2, 64, 3], replicated, may hold values from 0 to 1, as said below
Outputs:
- attended: bfloat16 [2, 2, 16384, 1536], P('tower', 'rep', 'seq')
- query_grad: bfloat16 [2, 2, 16384, 1536], P('tower', 'rep', 'seq')
- key_grad: bfloat16 [2, 2, 16384, 1536], P('tower', 'rep', 'seq')
- value_grad: bfloat16 [2, 2, 16384, 1536], P('tower', 'rep', 'seq')
- gain_grad: float32 [2, 1536], P('tower')
Inputs may be any that keep to these rules, and one draw needn't show every extreme that they name: `live_counts`: block 0 of each tower has 256 live tokens and block 1 has 128. `intersection`: every block intersections the other tower's block of the same index; the flags at offsets -1 and +1 vary.
All inputs are finite; a program needn't handle non-finite values.
Results may differ from a plain program's by a relative error of at most 0.0071.
Values may be sent and summed in bfloat16 or wider, within the bound.
A program may use at most 128 MiB of HBM per device.

v0:
```python
import functools
import math

import jax
import jax.numpy as jnp
from jax import lax
from jax.experimental import pallas as pl
from jax.experimental.pallas import tpu as pltpu
from jax.sharding import PartitionSpec as P

HEADS = 12
DIM = 128
TOK = 256
BLOCKS = 64
WIDE = 3 * TOK
WIDTH = HEADS * DIM
SCALE = 1.0 / math.sqrt(DIM)
PARTS = 2 * HEADS
AHEAD = 1
LAGS = (0, 1, 2, 3, 4)
EARLY = 2
VMEM_MIB = 60
MESH = pl.DeviceIdType.MESH
BF = jnp.bfloat16
F32 = jnp.float32


def dot(a, b, ca, cb):
    return lax.dot_general(a, b, (((ca,), (cb,)), ((), ())), preferred_element_type=F32)


def kernel(
    q_hbm, k_hbm, v_hbm, g_hbm, gain_hbm, counts_hbm, flags_hbm,
    att_hbm, dq_hbm, dk_hbm, dv_hbm, gg_ref,
    q_buf, g_buf, gain_ref, counts_ref, flags_ref, wide, rel_in, term_out, term_in, term_mid, total,
    part_in, cross_in, rel_total, probs_buf, low_buf, q_scaled, att_buf, dq_buf, gsum, gred,
    load_sem, swap_send, rel_recv, relay_send, kv_recv, fwd_send,
    term_send, term_recv, part_send, part_recv, cross_recv,
    fin_send, fin_recv, store_sem, gain_send, gain_recv,
):
    tower = lax.axis_index("tower")
    seq = lax.axis_index("seq")
    rep = lax.axis_index("rep")
    x_at, z_at, y_at = seq // 16, (seq // 4) % 4, seq % 4

    first = y_at == 0
    outer = first | (y_at == 3)
    inner = jnp.logical_not(outer)
    side = jnp.where(first, 3, 1)
    toward = jnp.where(first, BLOCKS - 1, 1)
    fwd_slot = jnp.where(first, 0, 2)
    cross_slot = 2 - fwd_slot
    cross_side = jnp.where(first, 0, 1)
    in_side = 1 - cross_side

    early_home = (first & (z_at == 0)) | ((y_at == 3) & (z_at == 3))
    early_relay = (first & (z_at == 3)) | ((y_at == 3) & (z_at == 0))
    home_shift = jnp.where(early_home, EARLY, 0)

    def shifted(block, step):
        return (block + step) % BLOCKS

    def along_z(block, step):
        return (block // 16) * 16 + ((block // 4 + step) % 4) * 4 + block % 4

    partner = (1 - tower, seq, rep)
    below = (tower, shifted(seq, BLOCKS - 1), rep)
    above = (tower, shifted(seq, 1), rep)
    my_relay = along_z(seq, side)
    relayed = along_z(seq, 4 - side)
    far_relay = (1 - tower, my_relay, rep)
    near_relay = (tower, my_relay, rep)
    relayed_home = (1 - tower, relayed, rep)
    relayed_query = (tower, relayed, rep)
    relayed_next = (tower, shifted(relayed, toward), rep)
    inside_next = (tower, shifted(seq, BLOCKS - toward), rep)
    term_relay = (tower, along_z(shifted(seq, toward), 4 - side), rep)

    group = (8, 4, 4)
    place = (y_at * 2 + rep, x_at, z_at)

    def along(axis, step):
        if axis == 0:
            spot = (place[0] + step) % 8
            return (tower, x_at * 16 + z_at * 4 + spot // 2, spot % 2)
        if axis == 1:
            return (tower, ((x_at + step) % 4) * 16 + z_at * 4 + y_at, rep)
        return (tower, along_z(seq, step), rep)

    loads = [
        pltpu.make_async_copy(q_hbm, q_buf, load_sem.at[0]),
        pltpu.make_async_copy(g_hbm, g_buf, load_sem.at[1]),
        pltpu.make_async_copy(gain_hbm, gain_ref, load_sem.at[2]),
        pltpu.make_async_copy(counts_hbm, counts_ref, load_sem.at[3]),
        pltpu.make_async_copy(flags_hbm, flags_ref, load_sem.at[4]),
    ]
    for copy in loads:
        copy.start()

    barrier = pltpu.get_barrier_semaphore()

    def greet(devices):
        for device in devices:
            pl.semaphore_signal(barrier, inc=1, device_id=device, device_id_type=MESH)
        pl.semaphore_wait(barrier, len(devices))

    everyone = []
    for axis in range(len(group)):
        everyone += [along(axis, step) for step in range(1, group[axis])]

    @pl.when(inner)
    def _():
        greet(everyone + [partner, below, above])

    @pl.when(outer)
    def _():
        greet(
            everyone
            + [inside_next, far_relay, near_relay, relayed_home]
            + [relayed_query, relayed_next, term_relay]
        )

    def columns(h):
        return pl.ds(h * DIM if isinstance(h, int) else pl.multiple_of(h * DIM, DIM), DIM)

    def remote(src, dst, send, recv, device):
        return pltpu.make_async_remote_copy(
            src_ref=src,
            dst_ref=dst,
            send_sem=send,
            recv_sem=recv,
            device_id=device,
            device_id_type=MESH,
        )

    sources = (k_hbm, v_hbm)
    targets = (dk_hbm, dv_hbm)

    def swap_copy(h, i):
        return remote(
            sources[i].at[:, columns(h)], wide.at[h, 1, i],
            swap_send.at[i], kv_recv.at[h, 1, i], partner,
        )

    def first_copy(h, i):
        return remote(
            sources[i].at[:, columns(h)], rel_in.at[h, i],
            swap_send.at[i], rel_recv.at[h, i], far_relay,
        )

    def relay_copies(h, i):
        return [
            remote(
                rel_in.at[h, i], wide.at[h, 1, i],
                relay_send.at[0], kv_recv.at[h, 1, i], relayed_query,
            ),
            remote(
                rel_in.at[h, i], wide.at[h, cross_slot, i],
                relay_send.at[1], kv_recv.at[h, cross_slot, i], relayed_next,
            ),
        ]

    def forward_both(h, i):
        return [
            remote(
                wide.at[h, 1, i], wide.at[h, j, i],
                fwd_send.at[j // 2], kv_recv.at[h, j, i], device,
            )
            for j, device in ((2, below), (0, above))
        ]

    def forward_inside(h, i):
        return [
            remote(
                wide.at[h, 1, i], wide.at[h, fwd_slot, i],
                fwd_send.at[0], kv_recv.at[h, fwd_slot, i], inside_next,
            )
        ]

    def terms_both(h, i):
        return [
            remote(
                term_out.at[h, j, i], term_in.at[h, j, i],
                term_send.at[j], term_recv.at[h, j, i], device,
            )
            for j, device in ((0, below), (1, above))
        ]

    def term_inside(h, i):
        return remote(
            term_out.at[h, in_side, i], term_in.at[h, in_side, i],
            term_send.at[0], term_recv.at[h, in_side, i], inside_next,
        )

    def term_cross(h, i):
        return remote(
            term_out.at[h, cross_side, i], cross_in.at[h, i],
            term_send.at[1], cross_recv.at[h, i], term_relay,
        )

    def term_arrival(h, i):
        return remote(
            term_out.at[h, 0, i], term_in.at[h, cross_side, i],
            term_send.at[0], term_recv.at[h, cross_side, i], inside_next,
        )

    def part_copy(h, i):
        return remote(
            total.at[h, i], part_in.at[h, i],
            part_send.at[0], part_recv.at[h, i], near_relay,
        )

    def final_copy(h, i, src, device):
        return remote(
            src.at[h, i], targets[i].at[:, columns(h)],
            fin_send.at[0], fin_recv.at[i], device,
        )

    def store_copies(h):
        return [
            pltpu.make_async_copy(att_buf.at[h], att_hbm.at[:, columns(h)], store_sem.at[0]),
            pltpu.make_async_copy(dq_buf.at[h], dq_hbm.at[:, columns(h)], store_sem.at[1]),
        ]

    def begin(copies):
        for copy in copies:
            copy.start()

    def arrived(copies):
        for copy in copies:
            copy.wait_recv()

    def sent(copies):
        for copy in copies:
            copy.wait_send()

    def either(relaying, direct):
        pl.when(outer)(relaying)
        pl.when(inner)(direct)

    def send_home(h, i):
        either(lambda: first_copy(h, i).start(), lambda: swap_copy(h, i).start())

    for part in range(AHEAD):
        send_home(part // 2, part % 2)

    @pl.when(early_home)
    def _():
        for part in range(AHEAD, AHEAD + 2 * EARLY):
            first_copy(part // 2, part % 2).start()

    for copy in loads:
        copy.wait()

    position = lax.broadcasted_iota(jnp.int32, (1, TOK), 1)
    bias = []
    for j in range(3):
        neighbour = seq + (j - 1)
        inside = jnp.clip(neighbour, 0, BLOCKS - 1)
        open_ = (neighbour == inside) & (flags_ref[j, tower, seq] == 1)
        live = jnp.where(open_, counts_ref[1 - tower, inside], 0)
        bias.append(jnp.where(position < live, 0.0, -1e30).astype(F32))
    bias = jnp.concatenate(bias, axis=1)
    gsum[...] = jnp.zeros_like(gsum)

    def relay(h, i):
        @pl.when(outer)
        def _():
            first_copy(h, i).wait_recv()
            begin(relay_copies(h, i))

    def forward(h, i):
        swap_copy(h, i).wait_recv()
        either(lambda: begin(forward_inside(h, i)), lambda: begin(forward_both(h, i)))

    def send_terms(h, i, left, right):
        terms = dot(left, right, 0, 0).astype(BF)
        term_out[h, 0, i] = terms[:TOK]
        term_mid[h, i] = terms[TOK : 2 * TOK]
        term_out[h, 1, i] = terms[2 * TOK :]
        either(
            lambda: begin([term_inside(h, i), term_cross(h, i)]),
            lambda: begin(terms_both(h, i)),
        )

    def compute(h, i):
        arrived(forward_both(h, i))
        gain = gain_ref[:, columns(h)]
        g = g_buf[:, columns(h)]
        if i == 0:
            q = (q_buf[:, columns(h)].astype(F32) * gain).astype(BF)
            q_scaled[...] = q
            keys = wide[h, :, 0].reshape(WIDE, DIM)
            scores = dot(q, keys, 1, 1) * SCALE + bias
            highest = jnp.max(scores, axis=1, keepdims=True)
            expo = jnp.exp(scores - highest)
            probs = expo / jnp.sum(expo, axis=1, keepdims=True)
            probs_buf[...] = probs
            low = probs.astype(BF)
            low_buf[...] = low
            send_terms(h, 1, low, g)
        else:
            keys = wide[h, :, 0].reshape(WIDE, DIM)
            values = wide[h, :, 1].reshape(WIDE, DIM)
            probs = probs_buf[...]
            dprob = dot(g, values, 1, 1)
            center = jnp.sum(probs * dprob, axis=1, keepdims=True)
            dscore = (probs * (dprob - center) * SCALE).astype(BF)
            send_terms(h, 0, dscore, q_scaled[...])
            att_buf[h] = dot(low_buf[...], values, 1, 0).astype(BF)
            dscaled = dot(dscore, keys, 1, 0)
            dq_buf[h] = (dscaled * gain).astype(BF)
            q_raw = q_buf[:, columns(h)].astype(F32)
            gsum[pl.ds(h, 1), :] = jnp.sum(q_raw * dscaled, axis=0, keepdims=True)
            begin(store_copies(h))

    def gather(h, part):
        i = 1 - part

        def relaying():
            term_arrival(h, i).wait_recv()
            total[h, i] = (
                term_mid[h, i].astype(F32) + term_in[h, cross_side, i].astype(F32)
            ).astype(BF)
            part_copy(h, i).start()

        def direct():
            arrived(terms_both(h, i))
            total[h, i] = (
                term_mid[h, i].astype(F32)
                + term_in[h, 0, i].astype(F32)
                + term_in[h, 1, i].astype(F32)
            ).astype(BF)
            final_copy(h, i, total, partner).start()

        either(relaying, direct)

    def pass_on(h, part):
        i = 1 - part

        @pl.when(outer)
        def _():
            part_copy(h, i).wait_recv()
            term_cross(h, i).wait_recv()
            rel_total[h, i] = (
                part_in[h, i].astype(F32) + cross_in[h, i].astype(F32)
            ).astype(BF)
            final_copy(h, i, rel_total, relayed_home).start()

    def relay_early(step, half):
        @pl.when(early_relay & (step < EARLY))
        def _():
            for i in range(2):
                relay(2 * step + half, i)

        @pl.when(early_relay & (step >= EARLY) & (step < HEADS - EARLY))
        def _():
            relay(step + EARLY, half)

    stages = (forward, compute, gather, pass_on)

    def advance(step, half):
        if not isinstance(step, int):
            h = step + (half + AHEAD) // 2 + home_shift
            pl.when(h < HEADS)(functools.partial(send_home, h, (half + AHEAD) % 2))
            relay_early(step, half)
            pl.when(jnp.logical_not(early_relay) & (step < HEADS))(
                functools.partial(relay, step, half)
            )
        for stage, lag in zip(stages, LAGS[1:]):
            h = step + (half - lag) // 2
            part = (half - lag) % 2
            if isinstance(h, int):
                if 0 <= h < HEADS:
                    stage(h, part)
            else:
                pl.when((h >= 0) & (h < HEADS))(functools.partial(stage, h, part))

    looped = (PARTS + LAGS[2] + 1) // 2

    @pl.loop(0, looped)
    def _(step):
        advance(step, 0)
        advance(step, 1)

    def gain_copies(axis):
        return [
            remote(
                gred.at[axis, place[axis]], gred.at[axis, place[axis]],
                gain_send.at[axis, step], gain_recv.at[axis, step], along(axis, step),
            )
            for step in range(1, group[axis])
        ]

    def gain_arrivals(axis):
        return [
            remote(
                gred.at[axis, 0],
                gred.at[axis, (place[axis] + group[axis] - step) % group[axis]],
                gain_send.at[axis, step], gain_recv.at[axis, step], along(axis, step),
            )
            for step in range(1, group[axis])
        ]

    def gain_begin(axis, part):
        gred[axis, place[axis]] = part
        begin(gain_copies(axis))

    def gain_end(axis):
        arrived(gain_arrivals(axis))
        part = gred[axis, 0]
        for slot in range(1, group[axis]):
            part = part + gred[axis, slot]
        return part

    gain_begin(0, gsum[...])
    ended = 0
    for part in range(2 * looped, PARTS + LAGS[4]):
        advance(part // 2, part % 2)
        if ended < 2 and part > 2 * looped:
            gain_begin(ended + 1, gain_end(ended))
            ended += 1
    for axis in range(ended, 2):
        gain_begin(axis + 1, gain_end(axis))

    def all_sent(ref, sems):
        for sem in sems:
            remote(ref, ref, sem, sem, partner).wait_send()

    all_sent(k_hbm, [swap_send.at[0], swap_send.at[1]])
    all_sent(total, [fwd_send.at[0], term_send.at[0], term_send.at[1], fin_send.at[0]])

    @pl.when(outer)
    def _():
        all_sent(total, [relay_send.at[0], relay_send.at[1], part_send.at[0]])

    @pl.when(inner)
    def _():
        all_sent(total, [fwd_send.at[1]])

    for i in range(2):
        pltpu.make_async_copy(att_buf, dq_buf, store_sem.at[i]).wait()

    for i in range(2):
        remote(k_hbm, targets[i], fin_send.at[0], fin_recv.at[i], partner).wait_recv()

    part = gain_end(2)
    for h in range(HEADS):
        gg_ref[:, h * DIM : (h + 1) * DIM] = part[h : h + 1]
    for axis in range(len(group)):
        sent(gain_copies(axis))


def keep(*refs):
    copies = []
    for i in range(4):
        for half in range(2):
            rows = pl.ds(half * 128, 128)
            held = refs[10].at[i, rows]
            copies.append(
                (
                    pltpu.make_async_copy(refs[i].at[rows], held, refs[11].at[0, i, half]),
                    pltpu.make_async_copy(held, refs[i + 5].at[rows], refs[11].at[1, i, half]),
                )
            )
    copies.append(
        (
            pltpu.make_async_copy(refs[4], refs[12], refs[13].at[0]),
            pltpu.make_async_copy(refs[12], refs[9], refs[13].at[1]),
        )
    )
    for load, _ in copies:
        load.start()
    for load, store in copies:
        load.wait()
        store.start()
    for _, store in copies:
        store.wait()


def per_device(query_rows, key_rows, value_rows, out_grad, query_gain, live_counts, intersection):
    anywhere = pl.BlockSpec(memory_space=pl.ANY)
    vmem = pl.BlockSpec(memory_space=pltpu.VMEM)
    block = jax.ShapeDtypeStruct((TOK, WIDTH), BF)
    dma = pltpu.SemaphoreType.DMA
    pair = (HEADS, 2)
    quad = (HEADS, 2, 2)
    shapes = (block, block, block, block, jax.ShapeDtypeStruct((1, WIDTH), F32))
    results = pl.pallas_call(
        kernel,
        out_shape=shapes,
        in_specs=[anywhere] * 7,
        out_specs=(anywhere,) * 4 + (vmem,),
        scratch_shapes=[
            pltpu.VMEM((TOK, WIDTH), BF),
            pltpu.VMEM((TOK, WIDTH), BF),
            pltpu.VMEM((1, WIDTH), F32),
            pltpu.SMEM((2, BLOCKS), jnp.int32),
            pltpu.SMEM((3, 2, BLOCKS), jnp.int32),
            pltpu.VMEM((HEADS, 3, 2, TOK, DIM), BF),
            pltpu.VMEM((HEADS, 2, TOK, DIM), BF),
            pltpu.VMEM((HEADS, 2, 2, TOK, DIM), BF),
            pltpu.VMEM((HEADS, 2, 2, TOK, DIM), BF),
            pltpu.VMEM((HEADS, 2, TOK, DIM), BF),
            pltpu.VMEM((HEADS, 2, TOK, DIM), BF),
            pltpu.VMEM((HEADS, 2, TOK, DIM), BF),
            pltpu.VMEM((HEADS, 2, TOK, DIM), BF),
            pltpu.VMEM((HEADS, 2, TOK, DIM), BF),
            pltpu.VMEM((TOK, WIDE), F32),
            pltpu.VMEM((TOK, WIDE), BF),
            pltpu.VMEM((TOK, DIM), BF),
            pltpu.VMEM((HEADS, TOK, DIM), BF),
            pltpu.VMEM((HEADS, TOK, DIM), BF),
            pltpu.VMEM((16, DIM), F32),
            pltpu.VMEM((3, 8, 16, DIM), F32),
            dma((5,)), dma((2,)), dma(pair), dma((2,)), dma((HEADS, 3, 2)), dma((2,)),
            dma((2,)), dma(quad), dma((1,)), dma(pair), dma(pair),
            dma((1,)), dma((2,)), dma((2,)), dma((3, 8)), dma((3, 8)),
        ],
        compiler_params=pltpu.CompilerParams(
            collective_id=0, has_side_effects=True, vmem_limit_bytes=VMEM_MIB * 2**20
        ),
        name="cross_attention",
    )(
        query_rows[0, 0], key_rows[0, 0], value_rows[0, 0], out_grad[0, 0],
        query_gain, live_counts, jnp.transpose(intersection, (2, 0, 1)),
    )
    results = pl.pallas_call(
        keep,
        out_shape=shapes,
        in_specs=[anywhere] * 5,
        out_specs=(anywhere,) * 5,
        scratch_shapes=[
            pltpu.VMEM((4, TOK, WIDTH), BF), dma((2, 4, 2)),
            pltpu.VMEM((1, WIDTH), F32), dma((2,)),
        ],
        compiler_params=pltpu.CompilerParams(vmem_limit_bytes=VMEM_MIB * 2**20),
        name="keep",
    )(*results)
    shape = (1, 1, TOK, WIDTH)
    return tuple(r.reshape(shape) for r in results[:4]) + (results[4],)


def solution(mesh):
    rows = P("tower", "rep", "seq", None)
    return jax.shard_map(
        per_device,
        mesh=mesh,
        in_specs=(rows, rows, rows, rows, P("tower", None), P(), P()),
        out_specs=(rows, rows, rows, rows, P("tower", None)),
        check_vma=False,
    )
```

profile of v0, /device:TPU:1, one launch (start us, length us, event | category | flops | bytes accessed | tf_op | source)
XLA Modules:
  0.0 173.4 jit_solution(6599527125932122336)
XLA Ops:
  0.6 169.9 %cross_attention.1 = (bf16[256,1536]{1,0:T(8,128)(2,1)}, bf16[256,1536]{1,0:T(8,128)(2,1)}, bf16[256,1536]{1,0:T(8,128)(2,1)}, bf16[256,1536]{1,0:T(8,128)(2,1)}, f32[1,1536]{1,0:T(1,128)}) custom-call(bf16[256,1536]{1,0:T(8,128)(2,1)} %bitcast.9, bf16[256,1536]{1,0:T(8,128)(2,1)} %bitcast.10, bf16[256,1536]{1,0:T(8,128)(2,1)} %bitcast.11, ...), custom_call_target="tpu_custom_call" | custom-call | tf_op jit(solution)/shard_map/cross_attention/pallas_call | solution.py:489
  170.6 2.8 %keep.1 = (bf16[256,1536]{1,0:T(8,128)(2,1)}, bf16[256,1536]{1,0:T(8,128)(2,1)}, bf16[256,1536]{1,0:T(8,128)(2,1)}, bf16[256,1536]{1,0:T(8,128)(2,1)}, f32[1,1536]{1,0:T(1,128)}) custom-call(bf16[256,1536]{1,0:T(8,128)(2,1)} %get-tuple-element.15.refs_0_, bf16[256,1536]{1,0:T(8,128)(2,1)} %get-tuple-element.16.refs_1_, ...), custom_call_target="tpu_custom_call" | custom-call | tf_op jit(solution)/shard_map/keep/pallas_call | solution.py:528
where the time goes:
time: 175 us; the launch traced here: 173 us
  Pallas kernels  173 us (99%)
    pallas_call x1, Pallas kernels, per_device(): pl.pallas_call(kernel, out_shape=shapes, in_specs=[anywhere] * 7, out_spe...  170 us

commit v1 on v0

--- a/solution.py
+++ b/solution.py
@@ -18,7 +18,8 @@
 PARTS = 2 * HEADS
 AHEAD = 1
 LAGS = (0, 1, 2, 3, 4)
-EARLY = 2
+EARLY = 3
+LATE = 1
 VMEM_MIB = 60
 MESH = pl.DeviceIdType.MESH
 BF = jnp.bfloat16
@@ -31,9 +32,9 @@
 
 def kernel(
     q_hbm, k_hbm, v_hbm, g_hbm, gain_hbm, counts_hbm, flags_hbm,
-    att_hbm, dq_hbm, dk_hbm, dv_hbm, gg_ref,
+    att_hbm, dq_hbm, dk_hbm, dv_hbm, gg_hbm,
     q_buf, g_buf, gain_ref, counts_ref, flags_ref, wide, rel_in, term_out, term_in, term_mid, total,
-    part_in, cross_in, rel_total, probs_buf, low_buf, q_scaled, att_buf, dq_buf, gsum, gred,
+    part_in, cross_in, rel_total, probs_buf, low_buf, q_scaled, att_buf, dq_buf, gsum, gred, gg_ref,
     load_sem, swap_send, rel_recv, relay_send, kv_recv, fwd_send,
     term_send, term_recv, part_send, part_recv, cross_recv,
     fin_send, fin_recv, store_sem, gain_send, gain_recv,
@@ -56,6 +57,7 @@
     early_home = (first & (z_at == 0)) | ((y_at == 3) & (z_at == 3))
     early_relay = (first & (z_at == 3)) | ((y_at == 3) & (z_at == 0))
     home_shift = jnp.where(early_home, EARLY, 0)
+    pass_shift = jnp.where(early_relay, LATE, 0)
 
     def shifted(block, step):
         return (block + step) % BLOCKS
@@ -360,21 +362,30 @@
     stages = (forward, compute, gather, pass_on)
 
     def advance(step, half):
-        if not isinstance(step, int):
-            h = step + (half + AHEAD) // 2 + home_shift
-            pl.when(h < HEADS)(functools.partial(send_home, h, (half + AHEAD) % 2))
-            relay_early(step, half)
-            pl.when(jnp.logical_not(early_relay) & (step < HEADS))(
-                functools.partial(relay, step, half)
-            )
-        for stage, lag in zip(stages, LAGS[1:]):
+        h = step + (half + AHEAD) // 2 + home_shift
+        pl.when(h < HEADS)(functools.partial(send_home, h, (half + AHEAD) % 2))
+        relay_early(step, half)
+        pl.when(jnp.logical_not(early_relay) & (step < HEADS))(
+            functools.partial(relay, step, half)
+        )
+        for stage, lag in zip((forward, compute), LAGS[1:3]):
             h = step + (half - lag) // 2
-            part = (half - lag) % 2
-            if isinstance(h, int):
-                if 0 <= h < HEADS:
-                    stage(h, part)
+            pl.when((h >= 0) & (h < HEADS))(functools.partial(stage, h, (half - lag) % 2))
+        for stage, lag, shift in ((gather, LAGS[3], 0), (pass_on, LAGS[4], pass_shift)):
+            h = step + (half - lag) // 2 - shift
+            pl.when((h >= 0) & (h < HEADS))(functools.partial(stage, h, (half - lag) % 2))
+
+    def conclude(first_part):
+        for part in range(first_part - LAGS[3], PARTS):
+            gather(part // 2, part % 2)
+        yield
+        for part in range(first_part - LAGS[4] - 2 * LATE, PARTS):
+            run = functools.partial(pass_on, part // 2, part % 2)
+            if part < first_part - LAGS[4]:
+                pl.when(early_relay)(run)
             else:
-                pl.when((h >= 0) & (h < HEADS))(functools.partial(stage, h, part))
+                run()
+        yield
 
     looped = (PARTS + LAGS[2] + 1) // 2
 
@@ -414,13 +425,7 @@
         return part
 
     gain_begin(0, gsum[...])
-    ended = 0
-    for part in range(2 * looped, PARTS + LAGS[4]):
-        advance(part // 2, part % 2)
-        if ended < 2 and part > 2 * looped:
-            gain_begin(ended + 1, gain_end(ended))
-            ended += 1
-    for axis in range(ended, 2):
+    for axis, _ in enumerate(conclude(2 * looped)):
         gain_begin(axis + 1, gain_end(axis))
 
     def all_sent(ref, sems):
@@ -441,21 +446,25 @@
     for i in range(2):
         pltpu.make_async_copy(att_buf, dq_buf, store_sem.at[i]).wait()
 
-    for i in range(2):
-        remote(k_hbm, targets[i], fin_send.at[0], fin_recv.at[i], partner).wait_recv()
-
     part = gain_end(2)
     for h in range(HEADS):
         gg_ref[:, h * DIM : (h + 1) * DIM] = part[h : h + 1]
+    gg_copy = pltpu.make_async_copy(gg_ref, gg_hbm, load_sem.at[5])
+    gg_copy.start()
     for axis in range(len(group)):
         sent(gain_copies(axis))
+
+    for i in range(2):
+        remote(k_hbm, targets[i], fin_send.at[0], fin_recv.at[i], partner).wait_recv()
+
+    gg_copy.wait()
 
 
 def keep(*refs):
     copies = []
     for i in range(4):
-        for half in range(2):
-            rows = pl.ds(half * 128, 128)
+        for half in range(4):
+            rows = pl.ds(half * 64, 64)
             held = refs[10].at[i, rows]
             copies.append(
                 (
@@ -480,7 +489,6 @@
 
 def per_device(query_rows, key_rows, value_rows, out_grad, query_gain, live_counts, intersection):
     anywhere = pl.BlockSpec(memory_space=pl.ANY)
-    vmem = pl.BlockSpec(memory_space=pltpu.VMEM)
     block = jax.ShapeDtypeStruct((TOK, WIDTH), BF)
     dma = pltpu.SemaphoreType.DMA
     pair = (HEADS, 2)
@@ -490,7 +498,7 @@
         kernel,
         out_shape=shapes,
         in_specs=[anywhere] * 7,
-        out_specs=(anywhere,) * 4 + (vmem,),
+        out_specs=(anywhere,) * 5,
         scratch_shapes=[
             pltpu.VMEM((TOK, WIDTH), BF),
             pltpu.VMEM((TOK, WIDTH), BF),
@@ -513,7 +521,8 @@
             pltpu.VMEM((HEADS, TOK, DIM), BF),
             pltpu.VMEM((16, DIM), F32),
             pltpu.VMEM((3, 8, 16, DIM), F32),
-            dma((5,)), dma((2,)), dma(pair), dma((2,)), dma((HEADS, 3, 2)), dma((2,)),
+            pltpu.VMEM((1, WIDTH), F32),
+            dma((6,)), dma((2,)), dma(pair), dma((2,)), dma((HEADS, 3, 2)), dma((2,)),
             dma((2,)), dma(quad), dma((1,)), dma(pair), dma(pair),
             dma((1,)), dma((2,)), dma((2,)), dma((3, 8)), dma((3, 8)),
         ],
@@ -531,7 +540,7 @@
         in_specs=[anywhere] * 5,
         out_specs=(anywhere,) * 5,
         scratch_shapes=[
-            pltpu.VMEM((4, TOK, WIDTH), BF), dma((2, 4, 2)),
+            pltpu.VMEM((4, TOK, WIDTH), BF), dma((2, 4, 4)),
             pltpu.VMEM((1, WIDTH), F32), dma((2,)),
         ],
         compiler_params=pltpu.CompilerParams(vmem_limit_bytes=VMEM_MIB * 2**20),

time: 175 us -> 174 us (level)
  no operation moved by 1% of the time
where the time goes in v1:
time: 174 us; the launch traced here: 173 us
  Pallas kernels  172 us (99%)
    pallas_call x1, Pallas kernels, per_device(): pl.pallas_call(kernel, out_shape=shapes, in_specs=[anywhere] * 7, out_spe...  169 us

profile of v1, /device:TPU:1, one launch (start us, length us, event | category | flops | bytes accessed | tf_op | source)
XLA Modules:
  0.0 173.1 jit_solution(18356990487238921953)
XLA Ops:
  0.6 169.3 %cross_attention.1 = (bf16[256,1536]{1,0:T(8,128)(2,1)}, bf16[256,1536]{1,0:T(8,128)(2,1)}, bf16[256,1536]{1,0:T(8,128)(2,1)}, bf16[256,1536]{1,0:T(8,128)(2,1)}, f32[1,1536]{1,0:T(1,128)}) custom-call(bf16[256,1536]{1,0:T(8,128)(2,1)} %bitcast.9, bf16[256,1536]{1,0:T(8,128)(2,1)} %bitcast.10, bf16[256,1536]{1,0:T(8,128)(2,1)} %bitcast.11, ...), custom_call_target="tpu_custom_call" | custom-call | tf_op jit(solution)/shard_map/cross_attention/pallas_call | solution.py:497
  169.9 3.2 %keep.1 = (bf16[256,1536]{1,0:T(8,128)(2,1)}, bf16[256,1536]{1,0:T(8,128)(2,1)}, bf16[256,1536]{1,0:T(8,128)(2,1)}, bf16[256,1536]{1,0:T(8,128)(2,1)}, f32[1,1536]{1,0:T(1,128)}) custom-call(bf16[256,1536]{1,0:T(8,128)(2,1)} %get-tuple-element.15.refs_0_, bf16[256,1536]{1,0:T(8,128)(2,1)} %get-tuple-element.16.refs_1_, ...), custom_call_target="tpu_custom_call" | custom-call | tf_op jit(solution)/shard_map/keep/pallas_call | solution.py:537

commit v2 on v1

--- a/solution.py
+++ b/solution.py
@@ -16,7 +16,7 @@
 WIDTH = HEADS * DIM
 SCALE = 1.0 / math.sqrt(DIM)
 PARTS = 2 * HEADS
-AHEAD = 1
+AHEAD = 2
 LAGS = (0, 1, 2, 3, 4)
 EARLY = 3
 LATE = 1

time: 174 us -> 176 us (1.011)
  Pallas kernels: 172 us -> 174 us
where the time goes in v2:
time: 176 us; the launch traced here: 175 us
  Pallas kernels  174 us (99%)
    pallas_call x1, Pallas kernels, per_device(): pl.pallas_call(kernel, out_shape=shapes, in_specs=[anywhere] * 7, out_spe...  171 us

profile of v2, /device:TPU:1, one launch (start us, length us, event | category | flops | bytes accessed | tf_op | source)
XLA Modules:
  0.0 174.5 jit_solution(5674509455053650512)
XLA Ops:
  0.6 170.7 %cross_attention.1 = (bf16[256,1536]{1,0:T(8,128)(2,1)}, bf16[256,1536]{1,0:T(8,128)(2,1)}, bf16[256,1536]{1,0:T(8,128)(2,1)}, bf16[256,1536]{1,0:T(8,128)(2,1)}, f32[1,1536]{1,0:T(1,128)}) custom-call(bf16[256,1536]{1,0:T(8,128)(2,1)} %bitcast.9, bf16[256,1536]{1,0:T(8,128)(2,1)} %bitcast.10, bf16[256,1536]{1,0:T(8,128)(2,1)} %bitcast.11, ...), custom_call_target="tpu_custom_call" | custom-call | tf_op jit(solution)/shard_map/cross_attention/pallas_call | solution.py:497
  171.3 3.2 %keep.1 = (bf16[256,1536]{1,0:T(8,128)(2,1)}, bf16[256,1536]{1,0:T(8,128)(2,1)}, bf16[256,1536]{1,0:T(8,128)(2,1)}, bf16[256,1536]{1,0:T(8,128)(2,1)}, f32[1,1536]{1,0:T(1,128)}) custom-call(bf16[256,1536]{1,0:T(8,128)(2,1)} %get-tuple-element.15.refs_0_, bf16[256,1536]{1,0:T(8,128)(2,1)} %get-tuple-element.16.refs_1_, ...), custom_call_target="tpu_custom_call" | custom-call | tf_op jit(solution)/shard_map/keep/pallas_call | solution.py:537
